TPU v7x, 256 devices: a whole 4x4x8 slice. The times are simulated.
256 devices in a mesh: tm: 16 (over z, y_hi), space: 16 (over y_lo, x, core).
Axes of the slice: x: 4, y: 4 (y_hi: 2, y_lo: 2; y = y_hi * 2 + y_lo), z: 8, core: 2. Of those that a mesh axis runs over, the one named last changes fastest.
Arguments:
- forcing: float32 [32, 12, 32, 2048], P('tm', None, 'space'), may hold values from -8 to 8
- iterate: float32 [32, 12, 32, 2048], P('tm', None, 'space'), may hold values from -8 to 8
- initial_state: float32 [12, 32, 2048], P(None, 'space'), may hold values from -8 to 8
- damping: float32 [12, 32, 2048], P(None, 'space'), may hold values from 0.5 to 1.5
- mixing: float32 [12, 12], replicated, may hold values from -0.12 to 0.12, as said below
- stencil: float32 [26, 12], replicated, may hold values from 0 to 0.04
Outputs:
- updated: float32 [32, 12, 32, 2048], P('tm', None, 'space')
- defect_vector: float32 [32, 12, 32, 2048], P('tm', None, 'space')
Inputs may be any that keep to these rules, and one draw needn't show every extreme that they name: `mixing`: the diagonal entries lie between 0 and 0.1; the others between -0.12 and 0.12.
All inputs are finite; a program needn't handle non-finite values.
Results may differ from a plain program's by a relative error of at most 0.0003.
Values sent between devices are 32-bit elements; how exact they have to be, the bound alone decides.
A program may use at most 64 MiB of HBM per device.

v0:
```python
import functools

import jax
import jax.numpy as jnp
from jax import lax
from jax.experimental import pallas as pl
from jax.experimental.pallas import tpu as pltpu
from jax.sharding import PartitionSpec as P

NZ = 64
LANES = 128
wrap_weight = 0.05
MESH = pl.DeviceIdType.MESH
NG, GC = 3, 4


def kernel(
    f_ref, x_ref, init_ref, damp_ref, mix_ref, st_ref,
    upd_ref, def_ref,
    xb, xh, q, qh, ini, prev, a, ah, e, r, co, cc, ch, u, b, e2, r2, co2, c2,
    prev_sem, xh_send, xh_recv, qh_send, qh_recv, ah_send, ah_recv, ch_send, ch_recv,
    s_send, s_recv,
):
    groups = lax.axis_size("tm")
    t = lax.axis_index("tm")
    slabs = lax.axis_size("space")
    s = lax.axis_index("space")
    has_low, has_high = s > 0, s < slabs - 1

    barrier = pltpu.get_barrier_semaphore()
    for k in range(1, groups):
        pl.semaphore_signal(barrier, inc=1, device_id={"tm": lax.rem(t + k, groups)}, device_id_type=MESH)

    @pl.when(has_low)
    def _():
        pl.semaphore_signal(barrier, inc=1, device_id={"space": s - 1}, device_id_type=MESH)

    @pl.when(has_high)
    def _():
        pl.semaphore_signal(barrier, inc=1, device_id={"space": s + 1}, device_id_type=MESH)

    lane = lax.broadcasted_iota(jnp.int32, (16, LANES), 1)
    row = lax.broadcasted_iota(jnp.int32, (16, LANES), 0)
    depth = lane % NZ
    half = lane < NZ

    def plane(ref, *index):
        return ref[index].reshape(16, LANES)

    def z_shifts(p):
        before = jnp.where(depth == 0, 0.0, pltpu.roll(p, 1, 1))
        after = jnp.where(depth == NZ - 1, 0.0, pltpu.roll(p, LANES - 1, 1))
        return before, p, after

    def y_before(p):
        turned = pltpu.roll(p, NZ, 1)
        return jnp.where(half, jnp.where(row == 0, 0.0, pltpu.roll(turned, 1, 0)), turned)

    def y_after(p):
        turned = pltpu.roll(p, NZ, 1)
        return jnp.where(half, turned, jnp.where(row == 15, 0.0, pltpu.roll(turned, 15, 0)))

    def neighbours(sheets, channel):
        shifted = [z_shifts(p) for p in sheets]
        out = []
        for at in range(2):
            sums = []
            for oy in range(3):
                total = None
                for ox in range(3):
                    for oz in range(3):
                        place = ox * 9 + oy * 3 + oz
                        if place == 13:
                            continue
                        term = st_ref[place - (place > 13), channel] * shifted[at + ox][oz]
                        total = term if total is None else total + term
                sums.append(total)
            out.append(sums[1] + y_before(sums[0]) + y_after(sums[2]))
        return out

    def to_sides(buf, halo, send, recv, sem):
        def low():
            return pltpu.make_async_remote_copy(
                buf(0), halo(1), send.at[1, sem], recv.at[1, sem], device_id={"space": s - 1}, device_id_type=MESH
            )

        def high():
            return pltpu.make_async_remote_copy(
                buf(1), halo(0), send.at[0, sem], recv.at[0, sem], device_id={"space": s + 1}, device_id_type=MESH
            )

        def start():
            pl.when(has_low)(lambda: low().start())
            pl.when(has_high)(lambda: high().start())

        def wait_recv():
            pl.when(has_low)(lambda: high().wait_recv())
            pl.when(has_high)(lambda: low().wait_recv())

        def wait_send():
            pl.when(has_low)(lambda: low().wait_send())
            pl.when(has_high)(lambda: high().wait_send())

        return start, wait_recv, wait_send

    def x_sides(g):
        return to_sides(lambda x: xb.at[:, g, :, pl.ds(2 * x, 2)], lambda x: xh.at[x, :, g], xh_send, xh_recv, g)

    def q_sides():
        return to_sides(lambda x: q.at[:, :, pl.ds(2 * x, 2)], lambda x: qh.at[x], qh_send, qh_recv, 0)

    def a_sides(g):
        return to_sides(lambda x: a.at[:, g, :, pl.ds(2 * x, 2)], lambda x: ah.at[x, :, g], ah_send, ah_recv, g)

    def c_sides(g):
        return to_sides(lambda x: cc.at[g, :, pl.ds(2 * x, 2)], lambda x: ch.at[x, g], ch_send, ch_recv, g)

    def chunk(ref, g, owner):
        return ref.at[g, owner // 4, owner % 4]

    def gather(src, dst, stage, g):
        for k in range(1, groups):
            owner = lax.rem(t + k, groups)
            pltpu.make_async_remote_copy(
                chunk(src, g, owner), dst.at[g, t], s_send.at[stage, g], s_recv.at[stage, g],
                device_id={"tm": owner}, device_id_type=MESH,
            ).start()
        dst[g, t] = src[g, t // 4, t % 4]

    def scatter(src, dst, stage, g):
        for k in range(1, groups):
            to = lax.rem(t + k, groups)
            pltpu.make_async_remote_copy(
                src.at[g, to], chunk(dst, g, t), s_send.at[stage, g], s_recv.at[stage, g],
                device_id={"tm": to}, device_id_type=MESH,
            ).start()
        dst[g, t // 4, t % 4] = src[g, t]

    def await_all(stage, g, sem):
        some = r.at[g, pl.ds(0, groups - 1)]
        pltpu.make_async_copy(some, some, sem.at[stage, g]).wait()

    def solve(src, dst, g, first):
        rate = q[g, t // 4, t % 4]
        rate = rate * rate
        total, power = src[g, 0], rate
        for n in range(1, groups):
            total = rate * total + src[g, n]
            power = power * rate
        total = wrap_weight * total if first is None else first + wrap_weight * total
        carry = total / (1.0 - wrap_weight * power)
        for n in range(groups):
            dst[g, n] = carry
            if n < groups - 1:
                carry = rate * carry + src[g, n]

    def split(c, _):
        for n in range(2):
            for x in range(2):
                xb[n, c // GC, c % GC, pl.ds(2 * x, 2)] = x_ref[n, c, pl.ds(x, 16, 2), :].reshape(2, 8, LANES)
        return 0

    lax.fori_loop(0, NG * GC, split, 0)
    edges = has_low.astype(jnp.int32) + has_high.astype(jnp.int32)
    pl.semaphore_wait(barrier, groups - 1 + edges)

    for g in range(NG):
        x_sides(g)[0]()

    def previous():
        return pltpu.make_async_remote_copy(
            x_ref.at[1], prev, prev_sem.at[0], prev_sem.at[1], device_id={"tm": t + 1}, device_id_type=MESH
        )

    pl.when(t < groups - 1)(lambda: previous().start())

    def rates(c, _):
        g, i = c // GC, c % GC
        for x in range(2):
            gain = damp_ref[c, pl.ds(x, 16, 2), :] + mix_ref[c, c]
            q[g, i, pl.ds(2 * x, 2)] = (1.0 / (1.0 + gain)).reshape(2, 8, LANES)
            ini[g, i, pl.ds(2 * x, 2)] = init_ref[c, pl.ds(x, 16, 2), :].reshape(2, 8, LANES)
        return 0

    lax.fori_loop(0, NG * GC, rates, 0)
    q_sides()[0]()

    for side, exists in ((0, has_low), (1, has_high)):

        @pl.when(jnp.logical_not(exists))
        def _(side=side):
            xh[side] = jnp.zeros(xh.shape[1:], jnp.float32)
            qh[side] = jnp.zeros(qh.shape[1:], jnp.float32)
            ah[side] = jnp.zeros(ah.shape[1:], jnp.float32)
            ch[side] = jnp.zeros(ch.shape[1:], jnp.float32)

    keep = jnp.where(t < groups - 1, 1.0, 0.0)

    def defects(g, _):
        x_sides(g)[1]()

        def channel(i, _):
            c = g * GC + i
            parts = []
            for n in range(2):
                own = [plane(xb, n, g, i, pl.ds(2 * x, 2)) for x in range(2)]
                near = neighbours([plane(xh, 0, n, g, i), *own, plane(xh, 1, n, g, i)], c)
                for x in range(2):
                    applied = damp_ref[c, pl.ds(x, 16, 2), :] * own[x] - near[x]
                    for d in range(NG * GC):
                        applied = applied + mix_ref[c, d] * plane(xb, n, d // GC, d % GC, pl.ds(2 * x, 2))
                    parts.append((own[x], applied))
            for x in range(2):
                at = pl.ds(2 * x, 2)
                (x0, k0), (x1, k1) = parts[x], parts[2 + x]
                d0 = f_ref[0, c, pl.ds(x, 16, 2), :] - (x0 + k0)
                d1 = f_ref[1, c, pl.ds(x, 16, 2), :] - (x1 - x0 + k1)
                rate = plane(q, g, i, at)
                a0 = rate * d0
                a1 = rate * (a0 + d1)
                def_ref[0, c, pl.ds(x, 16, 2), :] = d0
                def_ref[1, c, pl.ds(x, 16, 2), :] = d1
                a[0, g, i, at] = a0.reshape(2, 8, LANES)
                a[1, g, i, at] = a1.reshape(2, 8, LANES)
                e[g, i, at] = (a1 + keep * x1).reshape(2, 8, LANES)
            return 0

        lax.fori_loop(0, GC, channel, 0)
        gather(e, r, 0, g)
        a_sides(g)[0]()
        return 0

    lax.fori_loop(0, NG, defects, 0)

    def carries(g, _):
        await_all(0, g, s_recv)
        solve(r, co, g, ini[g, t // 4, t % 4])
        scatter(co, cc, 1, g)
        return 0

    lax.fori_loop(0, NG, carries, 0)
    q_sides()[1]()

    def first_sweep(g, _):
        await_all(1, g, s_recv)
        c_sides(g)[0]()

        def channel(i, _):
            rate, carry = q[g, i], cc[g, i]
            moved = rate * carry
            u[0, g, i] = a[0, g, i] + moved
            u[1, g, i] = a[1, g, i] + rate * moved
            return 0

        lax.fori_loop(0, GC, channel, 0)
        return 0

    lax.fori_loop(0, NG, first_sweep, 0)

    def second_sweep(g, _):
        a_sides(g)[1]()
        c_sides(g)[1]()

        def channel(i, _):
            c = g * GC + i
            halos = []
            for side in range(2):
                rate = plane(qh, side, g, i)
                moved = rate * plane(ch, side, g, i)
                halos.append((plane(ah, side, 0, g, i) + moved, plane(ah, side, 1, g, i) + rate * moved))
            parts = []
            for n in range(2):
                own = [plane(u, n, g, i, pl.ds(2 * x, 2)) for x in range(2)]
                near = neighbours([halos[0][n], *own, halos[1][n]], c)
                for x in range(2):
                    value = near[x]
                    for d in range(NG * GC):
                        weight = jnp.where(c == d, 0.0, mix_ref[c, d])
                        value = value - weight * plane(u, n, d // GC, d % GC, pl.ds(2 * x, 2))
                    parts.append((own[x], value))
            for x in range(2):
                at = pl.ds(2 * x, 2)
                (u0, h0), (u1, h1) = parts[x], parts[2 + x]
                rate = plane(q, g, i, at)
                v0 = rate * h0
                v1 = rate * (v0 + h1)
                b[0, g, i, at] = (plane(xb, 0, g, i, at) + (u0 + v0)).reshape(2, 8, LANES)
                b[1, g, i, at] = (plane(xb, 1, g, i, at) + (u1 + v1)).reshape(2, 8, LANES)
                e2[g, i, at] = v1.reshape(2, 8, LANES)
            return 0

        lax.fori_loop(0, GC, channel, 0)
        gather(e2, r2, 2, g)
        return 0

    lax.fori_loop(0, NG, second_sweep, 0)

    def carries_2(g, _):
        await_all(2, g, s_recv)
        solve(r2, co2, g, None)
        scatter(co2, c2, 3, g)
        return 0

    lax.fori_loop(0, NG, carries_2, 0)

    @pl.when(t > 0)
    def _():
        previous().wait_recv()
        def_ref[0] = def_ref[0] + prev[...]

    @pl.when(t == 0)
    def _():
        def_ref[0] = def_ref[0] + init_ref[...]

    def finish(g, _):
        await_all(3, g, s_recv)

        def channel(i, _):
            for x in range(2):
                at = pl.ds(2 * x, 2)
                rate = plane(q, g, i, at)
                moved = rate * plane(c2, g, i, at)
                upd_ref[0, g * GC + i, pl.ds(x, 16, 2), :] = plane(b, 0, g, i, at) + moved
                upd_ref[1, g * GC + i, pl.ds(x, 16, 2), :] = plane(b, 1, g, i, at) + rate * moved
            return 0

        lax.fori_loop(0, GC, channel, 0)
        return 0

    lax.fori_loop(0, NG, finish, 0)

    pl.when(t < groups - 1)(lambda: previous().wait_send())
    q_sides()[2]()
    for g in range(NG):
        x_sides(g)[2]()
        a_sides(g)[2]()
        c_sides(g)[2]()
        for stage in range(4):
            await_all(stage, g, s_send)


def rows_of(value):
    lead = value.shape[:-2]
    value = value.reshape(lead + (2, 16, LANES))
    return jnp.swapaxes(value, -3, -2).reshape(lead + (32, LANES))


def planes_of(value):
    lead = value.shape[:-2]
    value = value.reshape(lead + (16, 2, LANES))
    return jnp.swapaxes(value, -3, -2).reshape(lead + (2, 16 * LANES))


def body(forcing, iterate, initial_state, damping, mixing, stencil):
    vmem = pl.BlockSpec(memory_space=pltpu.VMEM)
    smem = pl.BlockSpec(memory_space=pltpu.SMEM)

    def field(*lead):
        return pltpu.VMEM((*lead, NG, GC, 4, 8, LANES), jnp.float32)

    def face(*lead):
        return pltpu.VMEM((*lead, NG, GC, 2, 8, LANES), jnp.float32)

    slots = pltpu.VMEM((NG, 16, 8, LANES), jnp.float32)
    dma = pltpu.SemaphoreType.DMA
    updated, defect = pl.pallas_call(
        kernel,
        out_shape=[jax.ShapeDtypeStruct((2, NG * GC, 32, LANES), jnp.float32)] * 2,
        in_specs=[vmem] * 4 + [smem] * 2,
        out_specs=[vmem] * 2,
        scratch_shapes=[
            field(2), face(2, 2), field(), face(2), field(),
            pltpu.VMEM((NG * GC, 32, LANES), jnp.float32),
            field(2), face(2, 2),
            field(), slots, slots, field(), face(2),
            field(2), field(2),
            field(), slots, slots, field(),
            dma((2,)),
            dma((2, NG)), dma((2, NG)),
            dma((2, 1)), dma((2, 1)),
            dma((2, NG)), dma((2, NG)),
            dma((2, NG)), dma((2, NG)),
            dma((4, NG)), dma((4, NG)),
        ],
        compiler_params=pltpu.CompilerParams(
            collective_id=0, has_side_effects=True, vmem_limit_bytes=40 * 1024 * 1024
        ),
    )(rows_of(forcing), rows_of(iterate), rows_of(initial_state), rows_of(damping), mixing, stencil)
    return planes_of(updated), planes_of(defect)


def solution(mesh):
    return jax.shard_map(
        body,
        mesh=mesh,
        in_specs=(
            P("tm", None, "space", None),
            P("tm", None, "space", None),
            P(None, "space", None),
            P(None, "space", None),
            P(),
            P(),
        ),
        out_specs=(P("tm", None, "space", None), P("tm", None, "space", None)),
        check_vma=False,
    )
```

profile of v0, /device:TPU:8, one launch (start us, length us, event | category | flops | bytes accessed | tf_op | source)
XLA Modules:
  0.0 55.3 jit_solution(9331909155227105297)
XLA Ops:
  0.6 0.0 copy-start.4
  0.6 0.8 %copy.12.st_ref = f32[26,12]{1,0:T(8,128)S(1)} copy(f32[26,12]{0,1:T(8,128)} %param.11) | data formatting | bytes 2496 | tf_op args[5]
  1.4 0.0 copy-done.4
  1.4 0.0 copy-start
  1.4 1.0 %copy-done = f32[2,12,2,2048]{3,2,1,0:T(2,128)S(1)} copy-done((f32[2,12,2,2048]{3,2,1,0:T(2,128)S(1)}, f32[2,12,2,2048]{3,2,1,0:T(2,128)}, u32[]{:S(2)}) %copy-start) | copy-done | bytes 393240
  2.4 0.0 copy-start.1
  2.4 1.0 %copy-done.1 = f32[2,12,2,2048]{3,2,1,0:T(2,128)S(1)} copy-done((f32[2,12,2,2048]{3,2,1,0:T(2,128)S(1)}, f32[2,12,2,2048]{3,2,1,0:T(2,128)}, u32[]{:S(2)}) %copy-start.1) | copy-done | bytes 393240
  3.4 0.0 copy-start.2
  3.4 0.9 %copy-done.2 = f32[12,2,2048]{2,1,0:T(2,128)S(1)} copy-done((f32[12,2,2048]{2,1,0:T(2,128)S(1)}, f32[12,2,2048]{2,1,0:T(2,128)}, u32[]{:S(2)}) %copy-start.2) | copy-done | bytes 196632
  4.4 0.0 copy-start.3
  4.4 0.9 %copy-done.3 = f32[12,2,2048]{2,1,0:T(2,128)S(1)} copy-done((f32[12,2,2048]{2,1,0:T(2,128)S(1)}, f32[12,2,2048]{2,1,0:T(2,128)}, u32[]{:S(2)}) %copy-start.3) | copy-done | bytes 196632
  5.3 48.5 %shard_map.77 = (f32[2,12,32,128]{3,2,1,0:T(8,128)S(1)}, f32[2,12,32,128]{3,2,1,0:T(8,128)S(1)}) custom-call(f32[2,12,32,128]{3,2,1,0:T(8,128)S(1)} %bitcast.32, f32[2,12,32,128]{3,2,1,0:T(8,128)S(1)} %bitcast.33, f32[12,32,128]{2,1,0:T(8,128)S(1)} %bitcast.34, f32[12,32,128]{2,1,0:T(8,128)S(1)} %bitcast.35, f32[12,12]{1,0:T(8,128)S(1)} %copy-done.4, ...), custom_call_target="tpu_custom_call" | custom-call | tf_op jit(solution)/shard_map/pallas_call | solution.py:366
  53.8 0.7 %copy.17 = f32[2,12,2,2048]{3,2,1,0:T(2,128)} copy(f32[2,12,2,2048]{3,2,1,0:T(2,128)S(1)} %bitcast.31) | data formatting | bytes 786432
  54.6 0.7 %copy.18 = f32[2,12,2,2048]{3,2,1,0:T(2,128)} copy(f32[2,12,2,2048]{3,2,1,0:T(2,128)S(1)} %bitcast.30) | data formatting | bytes 786432
Async XLA Ops:
  0.6 0.8 %copy-start.4 = (f32[12,12]{1,0:T(8,128)S(1)}, f32[12,12]{1,0:T(8,128)}, u32[]{:S(2)}) copy-start(f32[12,12]{1,0:T(8,128)} %mix_ref.1) | copy-start | bytes 1732
  1.4 1.0 %copy-start = (f32[2,12,2,2048]{3,2,1,0:T(2,128)S(1)}, f32[2,12,2,2048]{3,2,1,0:T(2,128)}, u32[]{:S(2)}) copy-start(f32[2,12,2,2048]{3,2,1,0:T(2,128)} %param.6) | copy-start | bytes 1179652
  2.4 1.0 %copy-start.1 = (f32[2,12,2,2048]{3,2,1,0:T(2,128)S(1)}, f32[2,12,2,2048]{3,2,1,0:T(2,128)}, u32[]{:S(2)}) copy-start(f32[2,12,2,2048]{3,2,1,0:T(2,128)} %param.7) | copy-start | bytes 1179652
  3.4 0.9 %copy-start.2 = (f32[12,2,2048]{2,1,0:T(2,128)S(1)}, f32[12,2,2048]{2,1,0:T(2,128)}, u32[]{:S(2)}) copy-start(f32[12,2,2048]{2,1,0:T(2,128)} %param.8) | copy-start | bytes 589828
  4.4 0.9 %copy-start.3 = (f32[12,2,2048]{2,1,0:T(2,128)S(1)}, f32[12,2,2048]{2,1,0:T(2,128)}, u32[]{:S(2)}) copy-start(f32[12,2,2048]{2,1,0:T(2,128)} %param.9) | copy-start | bytes 589828
where the time goes:
time: 56 us; the launch traced here: 55.3 us
  Pallas kernels  48.5 us (87%)
  local copies, waits for them, and re-layouts  6.13 us (11%)
  between operations  0.65 us (1%)
    pallas_call x1, Pallas kernels, body(): pl.pallas_call(kernel, out_shape=[jax.ShapeDtypeStruct((2, NG * GC, 32, L...  48.5 us
    unnamed x13, local copies, waits for them, and re-layouts  6.13 us

commit v1 on v0

--- a/solution.py
+++ b/solution.py
@@ -15,9 +15,10 @@
 
 
 def kernel(
-    f_ref, x_ref, init_ref, damp_ref, mix_ref, st_ref,
+    f_hbm, x_hbm, init_hbm, damp_hbm, mix_ref, st_ref,
     upd_ref, def_ref,
-    xb, xh, q, qh, ini, prev, a, ah, e, r, co, cc, ch, u, b, e2, r2, co2, c2,
+    f_ref, x_ref, init_ref, damp_ref, load_sem,
+    part, mine, mine_send, mine_recv, xb, xh, q, qh, ini, prev, a, ah, e, r, co, cc, ch, u, b, e2, r2, co2, c2,
     prev_sem, xh_send, xh_recv, qh_send, qh_recv, ah_send, ah_recv, ch_send, ch_recv,
     s_send, s_recv,
 ):
@@ -27,17 +28,30 @@
     s = lax.axis_index("space")
     has_low, has_high = s > 0, s < slabs - 1
 
+    other = lax.rem(s + slabs // 2, slabs)
+    z, y = t // 2, t % 2
+    partners = [
+        lax.rem(z + dz, groups // 2) * 2 + (y + dy) % 2 for dz in (4, 3, 5, 2, 6, 1, 7, 0) for dy in range(2)
+    ]
+
     barrier = pltpu.get_barrier_semaphore()
-    for k in range(1, groups):
-        pl.semaphore_signal(barrier, inc=1, device_id={"tm": lax.rem(t + k, groups)}, device_id_type=MESH)
-
-    @pl.when(has_low)
-    def _():
-        pl.semaphore_signal(barrier, inc=1, device_id={"space": s - 1}, device_id_type=MESH)
-
-    @pl.when(has_high)
-    def _():
-        pl.semaphore_signal(barrier, inc=1, device_id={"space": s + 1}, device_id_type=MESH)
+
+    def greet(**device):
+        pl.semaphore_signal(barrier, inc=1, device_id=device, device_id_type=MESH)
+
+    for partner in partners:
+        greet(tm=partner, space=other)
+    pl.when(has_low)(lambda: greet(space=s - 1))
+    pl.when(has_high)(lambda: greet(space=s + 1))
+    pl.when(t > 0)(lambda: greet(tm=t - 1))
+    loads = [
+        pltpu.make_async_copy(src, dst, load_sem.at[i])
+        for i, (src, dst) in enumerate(
+            ((x_hbm, x_ref), (damp_hbm, damp_ref), (init_hbm, init_ref), (f_hbm, f_ref))
+        )
+    ]
+    for load in loads:
+        load.start()
 
     lane = lax.broadcasted_iota(jnp.int32, (16, LANES), 1)
     row = lax.broadcasted_iota(jnp.int32, (16, LANES), 0)
@@ -60,23 +74,20 @@
         turned = pltpu.roll(p, NZ, 1)
         return jnp.where(half, turned, jnp.where(row == 15, 0.0, pltpu.roll(turned, 15, 0)))
 
-    def neighbours(sheets, channel):
-        shifted = [z_shifts(p) for p in sheets]
-        out = []
-        for at in range(2):
-            sums = []
-            for oy in range(3):
-                total = None
-                for ox in range(3):
-                    for oz in range(3):
-                        place = ox * 9 + oy * 3 + oz
-                        if place == 13:
-                            continue
-                        term = st_ref[place - (place > 13), channel] * shifted[at + ox][oz]
-                        total = term if total is None else total + term
-                sums.append(total)
-            out.append(sums[1] + y_before(sums[0]) + y_after(sums[2]))
-        return out
+    def taps(sheets, channel):
+        shifted = [None if p is None else z_shifts(p) for p in sheets]
+        sums = []
+        for oy in range(3):
+            total = None
+            for ox in range(3):
+                for oz in range(3):
+                    place = ox * 9 + oy * 3 + oz
+                    if place == 13 or shifted[ox] is None:
+                        continue
+                    term = st_ref[channel, place - (place > 13)] * shifted[ox][oz]
+                    total = term if total is None else total + term
+            sums.append(total)
+        return sums[1] + y_before(sums[0]) + y_after(sums[2])
 
     def to_sides(buf, halo, send, recv, sem):
         def low():
@@ -119,29 +130,32 @@
         return ref.at[g, owner // 4, owner % 4]
 
     def gather(src, dst, stage, g):
-        for k in range(1, groups):
-            owner = lax.rem(t + k, groups)
+        for owner in partners:
             pltpu.make_async_remote_copy(
                 chunk(src, g, owner), dst.at[g, t], s_send.at[stage, g], s_recv.at[stage, g],
-                device_id={"tm": owner}, device_id_type=MESH,
+                device_id={"tm": owner, "space": other}, device_id_type=MESH,
             ).start()
-        dst[g, t] = src[g, t // 4, t % 4]
 
     def scatter(src, dst, stage, g):
-        for k in range(1, groups):
-            to = lax.rem(t + k, groups)
+        for to in partners:
             pltpu.make_async_remote_copy(
                 src.at[g, to], chunk(dst, g, t), s_send.at[stage, g], s_recv.at[stage, g],
-                device_id={"tm": to}, device_id_type=MESH,
+                device_id={"tm": to, "space": other}, device_id_type=MESH,
             ).start()
-        dst[g, t // 4, t % 4] = src[g, t]
+
+    def constants(i):
+        src = q if i == 0 else ini
+        return pltpu.make_async_remote_copy(
+            src.at[:, t // 4, t % 4], mine.at[i], mine_send.at[i], mine_recv.at[i],
+            device_id={"space": other}, device_id_type=MESH,
+        )
 
     def await_all(stage, g, sem):
-        some = r.at[g, pl.ds(0, groups - 1)]
+        some = r.at[g]
         pltpu.make_async_copy(some, some, sem.at[stage, g]).wait()
 
     def solve(src, dst, g, first):
-        rate = q[g, t // 4, t % 4]
+        rate = mine[0, g]
         rate = rate * rate
         total, power = src[g, 0], rate
         for n in range(1, groups):
@@ -160,20 +174,6 @@
                 xb[n, c // GC, c % GC, pl.ds(2 * x, 2)] = x_ref[n, c, pl.ds(x, 16, 2), :].reshape(2, 8, LANES)
         return 0
 
-    lax.fori_loop(0, NG * GC, split, 0)
-    edges = has_low.astype(jnp.int32) + has_high.astype(jnp.int32)
-    pl.semaphore_wait(barrier, groups - 1 + edges)
-
-    for g in range(NG):
-        x_sides(g)[0]()
-
-    def previous():
-        return pltpu.make_async_remote_copy(
-            x_ref.at[1], prev, prev_sem.at[0], prev_sem.at[1], device_id={"tm": t + 1}, device_id_type=MESH
-        )
-
-    pl.when(t < groups - 1)(lambda: previous().start())
-
     def rates(c, _):
         g, i = c // GC, c % GC
         for x in range(2):
@@ -182,8 +182,27 @@
             ini[g, i, pl.ds(2 * x, 2)] = init_ref[c, pl.ds(x, 16, 2), :].reshape(2, 8, LANES)
         return 0
 
+    loads[0].wait()
+    lax.fori_loop(0, NG * GC, split, 0)
+    loads[1].wait()
+    loads[2].wait()
     lax.fori_loop(0, NG * GC, rates, 0)
+    loads[3].wait()
+    edges = has_low.astype(jnp.int32) + has_high.astype(jnp.int32) + (t < groups - 1).astype(jnp.int32)
+    pl.semaphore_wait(barrier, groups + edges)
+
+    for g in range(NG):
+        x_sides(g)[0]()
+    constants(0).start()
+    constants(1).start()
     q_sides()[0]()
+
+    def previous():
+        return pltpu.make_async_remote_copy(
+            x_ref.at[1], prev, prev_sem.at[0], prev_sem.at[1], device_id={"tm": t + 1}, device_id_type=MESH
+        )
+
+    pl.when(t < groups - 1)(lambda: previous().start())
 
     for side, exists in ((0, has_low), (1, has_high)):
 
@@ -196,25 +215,34 @@
 
     keep = jnp.where(t < groups - 1, 1.0, 0.0)
 
+    def defects_inside(c, _):
+        g, i = c // GC, c % GC
+        for n in range(2):
+            own = [plane(xb, n, g, i, pl.ds(2 * x, 2)) for x in range(2)]
+            for x in range(2):
+                near = taps([None, *own] if x == 0 else [*own, None], c)
+                applied = damp_ref[c, pl.ds(x, 16, 2), :] * own[x] - near
+                for d in range(NG * GC):
+                    applied = applied + mix_ref[c, d] * plane(xb, n, d // GC, d % GC, pl.ds(2 * x, 2))
+                step = own[x] if n == 0 else own[x] - plane(xb, 0, g, i, pl.ds(2 * x, 2))
+                value = f_ref[n, c, pl.ds(x, 16, 2), :] - (step + applied)
+                part[n, g, i, pl.ds(2 * x, 2)] = value.reshape(2, 8, LANES)
+        return 0
+
+    lax.fori_loop(0, NG * GC, defects_inside, 0)
+
     def defects(g, _):
         x_sides(g)[1]()
 
         def channel(i, _):
             c = g * GC + i
-            parts = []
-            for n in range(2):
-                own = [plane(xb, n, g, i, pl.ds(2 * x, 2)) for x in range(2)]
-                near = neighbours([plane(xh, 0, n, g, i), *own, plane(xh, 1, n, g, i)], c)
-                for x in range(2):
-                    applied = damp_ref[c, pl.ds(x, 16, 2), :] * own[x] - near[x]
-                    for d in range(NG * GC):
-                        applied = applied + mix_ref[c, d] * plane(xb, n, d // GC, d % GC, pl.ds(2 * x, 2))
-                    parts.append((own[x], applied))
             for x in range(2):
                 at = pl.ds(2 * x, 2)
-                (x0, k0), (x1, k1) = parts[x], parts[2 + x]
-                d0 = f_ref[0, c, pl.ds(x, 16, 2), :] - (x0 + k0)
-                d1 = f_ref[1, c, pl.ds(x, 16, 2), :] - (x1 - x0 + k1)
+                d0, d1 = (
+                    plane(part, n, g, i, at)
+                    + taps([plane(xh, 0, n, g, i), None, None] if x == 0 else [None, None, plane(xh, 1, n, g, i)], c)
+                    for n in range(2)
+                )
                 rate = plane(q, g, i, at)
                 a0 = rate * d0
                 a1 = rate * (a0 + d1)
@@ -222,7 +250,7 @@
                 def_ref[1, c, pl.ds(x, 16, 2), :] = d1
                 a[0, g, i, at] = a0.reshape(2, 8, LANES)
                 a[1, g, i, at] = a1.reshape(2, 8, LANES)
-                e[g, i, at] = (a1 + keep * x1).reshape(2, 8, LANES)
+                e[g, i, at] = (a1 + keep * plane(xb, 1, g, i, at)).reshape(2, 8, LANES)
             return 0
 
         lax.fori_loop(0, GC, channel, 0)
@@ -231,10 +259,12 @@
         return 0
 
     lax.fori_loop(0, NG, defects, 0)
+    constants(0).wait_recv()
+    constants(1).wait_recv()
 
     def carries(g, _):
         await_all(0, g, s_recv)
-        solve(r, co, g, ini[g, t // 4, t % 4])
+        solve(r, co, g, mine[1, g])
         scatter(co, cc, 1, g)
         return 0
 
@@ -250,12 +280,28 @@
             moved = rate * carry
             u[0, g, i] = a[0, g, i] + moved
             u[1, g, i] = a[1, g, i] + rate * moved
+            for n in range(2):
+                own = [plane(u, n, g, i, pl.ds(2 * x, 2)) for x in range(2)]
+                for x in range(2):
+                    near = taps([None, *own] if x == 0 else [*own, None], g * GC + i)
+                    part[n, g, i, pl.ds(2 * x, 2)] = near.reshape(2, 8, LANES)
             return 0
 
         lax.fori_loop(0, GC, channel, 0)
         return 0
 
     lax.fori_loop(0, NG, first_sweep, 0)
+
+    def mixed(c, _):
+        g, i = c // GC, c % GC
+        for n in range(2):
+            value = part[n, g, i]
+            for d in range(NG * GC):
+                value = value - jnp.where(c == d, 0.0, mix_ref[c, d]) * u[n, d // GC, d % GC]
+            part[n, g, i] = value
+        return 0
+
+    lax.fori_loop(0, NG * GC, mixed, 0)
 
     def second_sweep(g, _):
         a_sides(g)[1]()
@@ -263,29 +309,21 @@
 
         def channel(i, _):
             c = g * GC + i
-            halos = []
-            for side in range(2):
-                rate = plane(qh, side, g, i)
-                moved = rate * plane(ch, side, g, i)
-                halos.append((plane(ah, side, 0, g, i) + moved, plane(ah, side, 1, g, i) + rate * moved))
-            parts = []
-            for n in range(2):
-                own = [plane(u, n, g, i, pl.ds(2 * x, 2)) for x in range(2)]
-                near = neighbours([halos[0][n], *own, halos[1][n]], c)
-                for x in range(2):
-                    value = near[x]
-                    for d in range(NG * GC):
-                        weight = jnp.where(c == d, 0.0, mix_ref[c, d])
-                        value = value - weight * plane(u, n, d // GC, d % GC, pl.ds(2 * x, 2))
-                    parts.append((own[x], value))
             for x in range(2):
                 at = pl.ds(2 * x, 2)
-                (u0, h0), (u1, h1) = parts[x], parts[2 + x]
+                rate = plane(qh, x, g, i)
+                moved = rate * plane(ch, x, g, i)
+                halos = (plane(ah, x, 0, g, i) + moved, plane(ah, x, 1, g, i) + rate * moved)
+                h0, h1 = (
+                    plane(part, n, g, i, at)
+                    + taps([halos[n], None, None] if x == 0 else [None, None, halos[n]], c)
+                    for n in range(2)
+                )
                 rate = plane(q, g, i, at)
                 v0 = rate * h0
                 v1 = rate * (v0 + h1)
-                b[0, g, i, at] = (plane(xb, 0, g, i, at) + (u0 + v0)).reshape(2, 8, LANES)
-                b[1, g, i, at] = (plane(xb, 1, g, i, at) + (u1 + v1)).reshape(2, 8, LANES)
+                b[0, g, i, at] = (plane(xb, 0, g, i, at) + (plane(u, 0, g, i, at) + v0)).reshape(2, 8, LANES)
+                b[1, g, i, at] = (plane(xb, 1, g, i, at) + (plane(u, 1, g, i, at) + v1)).reshape(2, 8, LANES)
                 e2[g, i, at] = v1.reshape(2, 8, LANES)
             return 0
 
@@ -331,6 +369,8 @@
 
     pl.when(t < groups - 1)(lambda: previous().wait_send())
     q_sides()[2]()
+    constants(0).wait_send()
+    constants(1).wait_send()
     for g in range(NG):
         x_sides(g)[2]()
         a_sides(g)[2]()
@@ -351,9 +391,21 @@
     return jnp.swapaxes(value, -3, -2).reshape(lead + (2, 16 * LANES))
 
 
+def write(upd_vmem, def_vmem, upd_ref, def_ref, sem):
+    copies = [
+        pltpu.make_async_copy(upd_vmem, upd_ref, sem.at[0]),
+        pltpu.make_async_copy(def_vmem, def_ref, sem.at[1]),
+    ]
+    for copy in copies:
+        copy.start()
+    for copy in copies:
+        copy.wait()
+
+
 def body(forcing, iterate, initial_state, damping, mixing, stencil):
     vmem = pl.BlockSpec(memory_space=pltpu.VMEM)
     smem = pl.BlockSpec(memory_space=pltpu.SMEM)
+    hbm = pl.BlockSpec(memory_space=pltpu.HBM)
 
     def field(*lead):
         return pltpu.VMEM((*lead, NG, GC, 4, 8, LANES), jnp.float32)
@@ -361,16 +413,22 @@
     def face(*lead):
         return pltpu.VMEM((*lead, NG, GC, 2, 8, LANES), jnp.float32)
 
+    def rows(*lead):
+        return pltpu.VMEM((*lead, NG * GC, 32, LANES), jnp.float32)
+
     slots = pltpu.VMEM((NG, 16, 8, LANES), jnp.float32)
     dma = pltpu.SemaphoreType.DMA
-    updated, defect = pl.pallas_call(
+    whole = [jax.ShapeDtypeStruct((2, NG * GC, 32, LANES), jnp.float32)] * 2
+    results = pl.pallas_call(
         kernel,
-        out_shape=[jax.ShapeDtypeStruct((2, NG * GC, 32, LANES), jnp.float32)] * 2,
-        in_specs=[vmem] * 4 + [smem] * 2,
+        out_shape=[pltpu.VMEM((2, NG * GC, 32, LANES), jnp.float32)] * 2,
+        in_specs=[hbm] * 4 + [smem] * 2,
         out_specs=[vmem] * 2,
         scratch_shapes=[
+            rows(2), rows(2), rows(), rows(), dma((4,)),
+            field(2), pltpu.VMEM((2, NG, 8, LANES), jnp.float32), dma((2,)), dma((2,)),
             field(2), face(2, 2), field(), face(2), field(),
-            pltpu.VMEM((NG * GC, 32, LANES), jnp.float32),
+            rows(),
             field(2), face(2, 2),
             field(), slots, slots, field(), face(2),
             field(2), field(2),
@@ -383,9 +441,12 @@
             dma((4, NG)), dma((4, NG)),
         ],
         compiler_params=pltpu.CompilerParams(
-            collective_id=0, has_side_effects=True, vmem_limit_bytes=40 * 1024 * 1024
+            collective_id=0, has_side_effects=True, vmem_limit_bytes=60 * 1024 * 1024
         ),
-    )(rows_of(forcing), rows_of(iterate), rows_of(initial_state), rows_of(damping), mixing, stencil)
+    )(rows_of(forcing), rows_of(iterate), rows_of(initial_state), rows_of(damping), mixing, stencil.T)
+    updated, defect = pl.pallas_call(
+        write, out_shape=whole, in_specs=[vmem] * 2, out_specs=[hbm] * 2, scratch_shapes=[dma((2,))]
+    )(*results)
     return planes_of(updated), planes_of(defect)
 
 

time: 56 us -> 53 us (0.946)
  the two profiles are of different devices: /device:TPU:8 before, /device:TPU:32 now
where the time goes in v1:
time: 53 us; the launch traced here: 52.8 us
  Pallas kernels  50.7 us (96%)
  local copies, waits for them, and re-layouts  1.49 us (3%)
  between operations  0.65 us (1%)
    pallas_call x1, Pallas kernels, body(): pl.pallas_call(kernel, out_shape=[pltpu.VMEM((2, NG * GC, 32, LANES), jnp...  48.7 us
    pallas_call x1, Pallas kernels, body(): pl.pallas_call(write, out_shape=whole, in_specs=[vmem] * 2, out_specs=[hb...  2 us
    unnamed x4, local copies, waits for them, and re-layouts  1.49 us

profile of v1, /device:TPU:32, one launch (start us, length us, event | category | flops | bytes accessed | tf_op | source)
XLA Modules:
  0.0 52.8 jit_solution(2462200847251706844)
XLA Ops:
  0.6 48.7 %shard_map.77 = (f32[2,12,32,128]{3,2,1,0:T(8,128)S(1)}, f32[2,12,32,128]{3,2,1,0:T(8,128)S(1)}) custom-call(f32[2,12,32,128]{3,2,1,0:T(8,128)} %bitcast.31, f32[2,12,32,128]{3,2,1,0:T(8,128)} %bitcast.32, f32[12,32,128]{2,1,0:T(8,128)} %bitcast.33, f32[12,32,128]{2,1,0:T(8,128)} %bitcast.34, f32[12,12]{1,0:T(8,128)} %mix_ref.1, f32[12,26]{1,0:T(8,128)} %bitcast.35), custom_call_target="tpu_custom_call" | custom-call | tf_op jit(solution)/shard_map/pallas_call | solution.py:422
  49.3 0.0 copy-start
  49.3 0.7 %copy-done = f32[2,12,32,128]{3,2,1,0:T(8,128)} copy-done((f32[2,12,32,128]{3,2,1,0:T(8,128)}, f32[2,12,32,128]{3,2,1,0:T(8,128)S(1)}, u32[]{:S(2)}) %copy-start) | copy-done | bytes 393240
  50.1 0.0 copy-start.1
  50.1 0.7 %copy-done.1 = f32[2,12,32,128]{3,2,1,0:T(8,128)} copy-done((f32[2,12,32,128]{3,2,1,0:T(8,128)}, f32[2,12,32,128]{3,2,1,0:T(8,128)S(1)}, u32[]{:S(2)}) %copy-start.1) | copy-done | bytes 393240
  50.8 2.0 %shard_map.78 = (f32[2,12,32,128]{3,2,1,0:T(8,128)}, f32[2,12,32,128]{3,2,1,0:T(8,128)}) custom-call(f32[2,12,32,128]{3,2,1,0:T(8,128)} %copy-done, f32[2,12,32,128]{3,2,1,0:T(8,128)} %copy-done.1), custom_call_target="tpu_custom_call" | custom-call | tf_op jit(solution)/shard_map/pallas_call | solution.py:447
Async XLA Ops:
  49.3 0.8 %copy-start = (f32[2,12,32,128]{3,2,1,0:T(8,128)}, f32[2,12,32,128]{3,2,1,0:T(8,128)S(1)}, u32[]{:S(2)}) copy-start(f32[2,12,32,128]{3,2,1,0:T(8,128)S(1)} %get-tuple-element.6.upd_vmem) | copy-start | bytes 1179652
  50.1 0.7 %copy-start.1 = (f32[2,12,32,128]{3,2,1,0:T(8,128)}, f32[2,12,32,128]{3,2,1,0:T(8,128)S(1)}, u32[]{:S(2)}) copy-start(f32[2,12,32,128]{3,2,1,0:T(8,128)S(1)} %get-tuple-element.7.def_vmem) | copy-start | bytes 1179652

commit v2 on v1

--- a/solution.py
+++ b/solution.py
@@ -12,14 +12,15 @@
 wrap_weight = 0.05
 MESH = pl.DeviceIdType.MESH
 NG, GC = 3, 4
+UNROLL = 4
 
 
 def kernel(
     f_hbm, x_hbm, init_hbm, damp_hbm, mix_ref, st_ref,
     upd_ref, def_ref,
     f_ref, x_ref, init_ref, damp_ref, load_sem,
-    part, mine, mine_send, mine_recv, xb, xh, q, qh, ini, prev, a, ah, e, r, co, cc, ch, u, b, e2, r2, co2, c2,
-    prev_sem, xh_send, xh_recv, qh_send, qh_recv, ah_send, ah_recv, ch_send, ch_recv,
+    part, aside, mine, mine_send, mine_recv, xb, xh, q, qh, ini, prev, a, ah, e, r, co, cc, ch, u, b, e2, r2, co2, c2,
+    prev_send, prev_recv, xh_send, xh_recv, qh_send, qh_recv, ah_send, ah_recv, ch_send, ch_recv,
     s_send, s_recv,
 ):
     groups = lax.axis_size("tm")
@@ -66,28 +67,28 @@
         after = jnp.where(depth == NZ - 1, 0.0, pltpu.roll(p, LANES - 1, 1))
         return before, p, after
 
-    def y_before(p):
-        turned = pltpu.roll(p, NZ, 1)
-        return jnp.where(half, jnp.where(row == 0, 0.0, pltpu.roll(turned, 1, 0)), turned)
-
-    def y_after(p):
-        turned = pltpu.roll(p, NZ, 1)
-        return jnp.where(half, turned, jnp.where(row == 15, 0.0, pltpu.roll(turned, 15, 0)))
-
-    def taps(sheets, channel):
-        shifted = [None if p is None else z_shifts(p) for p in sheets]
+    def sums_of(sheets, channel):
         sums = []
         for oy in range(3):
             total = None
             for ox in range(3):
                 for oz in range(3):
                     place = ox * 9 + oy * 3 + oz
-                    if place == 13 or shifted[ox] is None:
+                    if place == 13 or sheets[ox] is None:
                         continue
-                    term = st_ref[channel, place - (place > 13)] * shifted[ox][oz]
+                    term = st_ref[channel, place - (place > 13)] * sheets[ox][oz]
                     total = term if total is None else total + term
             sums.append(total)
-        return sums[1] + y_before(sums[0]) + y_after(sums[2])
+        before, here, after = sums
+        above = jnp.where(row == 15, 0.0, pltpu.roll(after, 15, 0))
+        below = jnp.where(row == 0, 0.0, pltpu.roll(before, 1, 0))
+        return here, jnp.where(half, before + above, below + after)
+
+    def turn(p):
+        return pltpu.roll(p, NZ, 1)
+
+    def tile(p):
+        return p.reshape(2, 8, LANES)
 
     def to_sides(buf, halo, send, recv, sem):
         def low():
@@ -195,14 +196,15 @@
         x_sides(g)[0]()
     constants(0).start()
     constants(1).start()
-    q_sides()[0]()
-
-    def previous():
+
+    def previous(h):
+        some = pl.ds(6 * h, 6)
         return pltpu.make_async_remote_copy(
-            x_ref.at[1], prev, prev_sem.at[0], prev_sem.at[1], device_id={"tm": t + 1}, device_id_type=MESH
+            x_ref.at[1, some], prev.at[some], prev_send.at[h], prev_recv.at[h],
+            device_id={"tm": t + 1}, device_id_type=MESH,
         )
 
-    pl.when(t < groups - 1)(lambda: previous().start())
+    pl.when(t < groups - 1)(lambda: previous(0).start())
 
     for side, exists in ((0, has_low), (1, has_high)):
 
@@ -219,17 +221,20 @@
         g, i = c // GC, c % GC
         for n in range(2):
             own = [plane(xb, n, g, i, pl.ds(2 * x, 2)) for x in range(2)]
+            moved = [z_shifts(p) for p in own]
             for x in range(2):
-                near = taps([None, *own] if x == 0 else [*own, None], c)
-                applied = damp_ref[c, pl.ds(x, 16, 2), :] * own[x] - near
+                at = pl.ds(2 * x, 2)
+                here, turned = sums_of([None, *moved] if x == 0 else [*moved, None], c)
+                value = f_ref[n, c, pl.ds(x, 16, 2), :] - own[x] - damp_ref[c, pl.ds(x, 16, 2), :] * own[x] + here
                 for d in range(NG * GC):
-                    applied = applied + mix_ref[c, d] * plane(xb, n, d // GC, d % GC, pl.ds(2 * x, 2))
-                step = own[x] if n == 0 else own[x] - plane(xb, 0, g, i, pl.ds(2 * x, 2))
-                value = f_ref[n, c, pl.ds(x, 16, 2), :] - (step + applied)
-                part[n, g, i, pl.ds(2 * x, 2)] = value.reshape(2, 8, LANES)
-        return 0
-
-    lax.fori_loop(0, NG * GC, defects_inside, 0)
+                    value = value - mix_ref[c, d] * plane(xb, n, d // GC, d % GC, at)
+                if n == 1:
+                    value = value + plane(xb, 0, g, i, at)
+                part[n, g, i, at] = tile(value)
+                aside[n, g, i, at] = tile(turned)
+        return 0
+
+    lax.fori_loop(0, NG * GC, defects_inside, 0, unroll=UNROLL)
 
     def defects(g, _):
         x_sides(g)[1]()
@@ -238,27 +243,30 @@
             c = g * GC + i
             for x in range(2):
                 at = pl.ds(2 * x, 2)
-                d0, d1 = (
-                    plane(part, n, g, i, at)
-                    + taps([plane(xh, 0, n, g, i), None, None] if x == 0 else [None, None, plane(xh, 1, n, g, i)], c)
-                    for n in range(2)
-                )
+                values = []
+                for n in range(2):
+                    moved = z_shifts(plane(xh, x, n, g, i))
+                    here, turned = sums_of([moved, None, None] if x == 0 else [None, None, moved], c)
+                    values.append(plane(part, n, g, i, at) + here + turn(plane(aside, n, g, i, at) + turned))
+                d0, d1 = values
                 rate = plane(q, g, i, at)
                 a0 = rate * d0
                 a1 = rate * (a0 + d1)
                 def_ref[0, c, pl.ds(x, 16, 2), :] = d0
                 def_ref[1, c, pl.ds(x, 16, 2), :] = d1
-                a[0, g, i, at] = a0.reshape(2, 8, LANES)
-                a[1, g, i, at] = a1.reshape(2, 8, LANES)
-                e[g, i, at] = (a1 + keep * plane(xb, 1, g, i, at)).reshape(2, 8, LANES)
+                a[0, g, i, at] = tile(a0)
+                a[1, g, i, at] = tile(a1)
+                e[g, i, at] = tile(a1 + keep * plane(xb, 1, g, i, at))
             return 0
 
-        lax.fori_loop(0, GC, channel, 0)
+        lax.fori_loop(0, GC, channel, 0, unroll=UNROLL)
         gather(e, r, 0, g)
+        return 0
+
+    lax.fori_loop(0, NG, defects, 0)
+    for g in range(NG):
         a_sides(g)[0]()
-        return 0
-
-    lax.fori_loop(0, NG, defects, 0)
+    q_sides()[0]()
     constants(0).wait_recv()
     constants(1).wait_recv()
 
@@ -269,7 +277,6 @@
         return 0
 
     lax.fori_loop(0, NG, carries, 0)
-    q_sides()[1]()
 
     def first_sweep(g, _):
         await_all(1, g, s_recv)
@@ -281,16 +288,19 @@
             u[0, g, i] = a[0, g, i] + moved
             u[1, g, i] = a[1, g, i] + rate * moved
             for n in range(2):
-                own = [plane(u, n, g, i, pl.ds(2 * x, 2)) for x in range(2)]
+                moved = [z_shifts(plane(u, n, g, i, pl.ds(2 * x, 2))) for x in range(2)]
                 for x in range(2):
-                    near = taps([None, *own] if x == 0 else [*own, None], g * GC + i)
-                    part[n, g, i, pl.ds(2 * x, 2)] = near.reshape(2, 8, LANES)
+                    at = pl.ds(2 * x, 2)
+                    here, turned = sums_of([None, *moved] if x == 0 else [*moved, None], g * GC + i)
+                    part[n, g, i, at] = tile(here)
+                    aside[n, g, i, at] = tile(turned)
             return 0
 
-        lax.fori_loop(0, GC, channel, 0)
+        lax.fori_loop(0, GC, channel, 0, unroll=UNROLL)
         return 0
 
     lax.fori_loop(0, NG, first_sweep, 0)
+    pl.when(t < groups - 1)(lambda: previous(1).start())
 
     def mixed(c, _):
         g, i = c // GC, c % GC
@@ -301,7 +311,8 @@
             part[n, g, i] = value
         return 0
 
-    lax.fori_loop(0, NG * GC, mixed, 0)
+    lax.fori_loop(0, NG * GC, mixed, 0, unroll=UNROLL)
+    q_sides()[1]()
 
     def second_sweep(g, _):
         a_sides(g)[1]()
@@ -314,20 +325,21 @@
                 rate = plane(qh, x, g, i)
                 moved = rate * plane(ch, x, g, i)
                 halos = (plane(ah, x, 0, g, i) + moved, plane(ah, x, 1, g, i) + rate * moved)
-                h0, h1 = (
-                    plane(part, n, g, i, at)
-                    + taps([halos[n], None, None] if x == 0 else [None, None, halos[n]], c)
-                    for n in range(2)
-                )
+                values = []
+                for n in range(2):
+                    moved = z_shifts(halos[n])
+                    here, turned = sums_of([moved, None, None] if x == 0 else [None, None, moved], c)
+                    values.append(plane(part, n, g, i, at) + here + turn(plane(aside, n, g, i, at) + turned))
+                h0, h1 = values
                 rate = plane(q, g, i, at)
                 v0 = rate * h0
                 v1 = rate * (v0 + h1)
-                b[0, g, i, at] = (plane(xb, 0, g, i, at) + (plane(u, 0, g, i, at) + v0)).reshape(2, 8, LANES)
-                b[1, g, i, at] = (plane(xb, 1, g, i, at) + (plane(u, 1, g, i, at) + v1)).reshape(2, 8, LANES)
-                e2[g, i, at] = v1.reshape(2, 8, LANES)
+                e2[g, i, at] = tile(v1)
+                b[0, g, i, at] = tile(plane(xb, 0, g, i, at) + (plane(u, 0, g, i, at) + v0))
+                b[1, g, i, at] = tile(plane(xb, 1, g, i, at) + (plane(u, 1, g, i, at) + v1))
             return 0
 
-        lax.fori_loop(0, GC, channel, 0)
+        lax.fori_loop(0, GC, channel, 0, unroll=UNROLL)
         gather(e2, r2, 2, g)
         return 0
 
@@ -343,7 +355,8 @@
 
     @pl.when(t > 0)
     def _():
-        previous().wait_recv()
+        previous(0).wait_recv()
+        previous(1).wait_recv()
         def_ref[0] = def_ref[0] + prev[...]
 
     @pl.when(t == 0)
@@ -367,7 +380,8 @@
 
     lax.fori_loop(0, NG, finish, 0)
 
-    pl.when(t < groups - 1)(lambda: previous().wait_send())
+    pl.when(t < groups - 1)(lambda: previous(0).wait_send())
+    pl.when(t < groups - 1)(lambda: previous(1).wait_send())
     q_sides()[2]()
     constants(0).wait_send()
     constants(1).wait_send()
@@ -391,17 +405,6 @@
     return jnp.swapaxes(value, -3, -2).reshape(lead + (2, 16 * LANES))
 
 
-def write(upd_vmem, def_vmem, upd_ref, def_ref, sem):
-    copies = [
-        pltpu.make_async_copy(upd_vmem, upd_ref, sem.at[0]),
-        pltpu.make_async_copy(def_vmem, def_ref, sem.at[1]),
-    ]
-    for copy in copies:
-        copy.start()
-    for copy in copies:
-        copy.wait()
-
-
 def body(forcing, iterate, initial_state, damping, mixing, stencil):
     vmem = pl.BlockSpec(memory_space=pltpu.VMEM)
     smem = pl.BlockSpec(memory_space=pltpu.SMEM)
@@ -418,22 +421,21 @@
 
     slots = pltpu.VMEM((NG, 16, 8, LANES), jnp.float32)
     dma = pltpu.SemaphoreType.DMA
-    whole = [jax.ShapeDtypeStruct((2, NG * GC, 32, LANES), jnp.float32)] * 2
-    results = pl.pallas_call(
+    updated, defect = pl.pallas_call(
         kernel,
-        out_shape=[pltpu.VMEM((2, NG * GC, 32, LANES), jnp.float32)] * 2,
+        out_shape=[rows(2)] * 2,
         in_specs=[hbm] * 4 + [smem] * 2,
         out_specs=[vmem] * 2,
         scratch_shapes=[
             rows(2), rows(2), rows(), rows(), dma((4,)),
-            field(2), pltpu.VMEM((2, NG, 8, LANES), jnp.float32), dma((2,)), dma((2,)),
+            field(2), field(2), pltpu.VMEM((2, NG, 8, LANES), jnp.float32), dma((2,)), dma((2,)),
             field(2), face(2, 2), field(), face(2), field(),
             rows(),
             field(2), face(2, 2),
             field(), slots, slots, field(), face(2),
             field(2), field(2),
             field(), slots, slots, field(),
-            dma((2,)),
+            dma((2,)), dma((2,)),
             dma((2, NG)), dma((2, NG)),
             dma((2, 1)), dma((2, 1)),
             dma((2, NG)), dma((2, NG)),
@@ -444,9 +446,6 @@
             collective_id=0, has_side_effects=True, vmem_limit_bytes=60 * 1024 * 1024
         ),
     )(rows_of(forcing), rows_of(iterate), rows_of(initial_state), rows_of(damping), mixing, stencil.T)
-    updated, defect = pl.pallas_call(
-        write, out_shape=whole, in_specs=[vmem] * 2, out_specs=[hbm] * 2, scratch_shapes=[dma((2,))]
-    )(*results)
     return planes_of(updated), planes_of(defect)
 
 

time: 53 us -> 46.4 us (0.88)
  the two profiles are of different devices: /device:TPU:32 before, /device:TPU:8 now
where the time goes in v2:
time: 46.4 us; the launch traced here: 45.8 us
  Pallas kernels  43.7 us (94%)
  local copies, waits for them, and re-layouts  1.49 us (3%)
  between operations  0.64 us (1%)
    pallas_call x1, Pallas kernels, body(): pl.pallas_call(kernel, out_shape=[rows(2)] * 2, in_specs=[hbm] * 4 + [sme...  43.7 us
    unnamed x2, local copies, waits for them, and re-layouts  1.49 us

profile of v2, /device:TPU:8, one launch (start us, length us, event | category | flops | bytes accessed | tf_op | source)
XLA Modules:
  0.0 45.8 jit_solution(15070660619843302379)
XLA Ops:
  0.6 43.7 %shard_map.77 = (f32[2,12,32,128]{3,2,1,0:T(8,128)S(1)}, f32[2,12,32,128]{3,2,1,0:T(8,128)S(1)}) custom-call(f32[2,12,32,128]{3,2,1,0:T(8,128)} %bitcast.33, f32[2,12,32,128]{3,2,1,0:T(8,128)} %bitcast.34, f32[12,32,128]{2,1,0:T(8,128)} %bitcast.35, f32[12,32,128]{2,1,0:T(8,128)} %bitcast.36, f32[12,12]{1,0:T(8,128)} %mix_ref.1, f32[12,26]{1,0:T(8,128)} %bitcast.37), custom_call_target="tpu_custom_call" | custom-call | tf_op jit(solution)/shard_map/pallas_call | solution.py:424
  44.3 0.7 %copy.16 = f32[2,12,2,2048]{3,2,1,0:T(2,128)} copy(f32[2,12,2,2048]{3,2,1,0:T(2,128)S(1)} %bitcast.32) | data formatting | bytes 786432
  45.1 0.7 %copy.17 = f32[2,12,2,2048]{3,2,1,0:T(2,128)} copy(f32[2,12,2,2048]{3,2,1,0:T(2,128)S(1)} %bitcast.31) | data formatting | bytes 786432

commit v3 on v2

--- a/solution.py
+++ b/solution.py
@@ -13,16 +13,18 @@
 MESH = pl.DeviceIdType.MESH
 NG, GC = 3, 4
 UNROLL = 4
+CUT = 6
 
 
 def kernel(
-    f_hbm, x_hbm, init_hbm, damp_hbm, mix_ref, st_ref,
-    upd_ref, def_ref,
-    f_ref, x_ref, init_ref, damp_ref, load_sem,
+    f_hbm, x_hbm, init_hbm, damp_hbm, mix_hbm, st_hbm,
+    out_ref,
+    f_ref, x_ref, init_ref, damp_ref, mix_ref, st_ref, load_sem, second, third,
     part, aside, mine, mine_send, mine_recv, xb, xh, q, qh, ini, prev, a, ah, e, r, co, cc, ch, u, b, e2, r2, co2, c2,
     prev_send, prev_recv, xh_send, xh_recv, qh_send, qh_recv, ah_send, ah_recv, ch_send, ch_recv,
     s_send, s_recv,
 ):
+    upd_ref, def_ref = out_ref.at[0], out_ref.at[1]
     groups = lax.axis_size("tm")
     t = lax.axis_index("tm")
     slabs = lax.axis_size("space")
@@ -36,19 +38,21 @@
     ]
 
     barrier = pltpu.get_barrier_semaphore()
-
-    def greet(**device):
-        pl.semaphore_signal(barrier, inc=1, device_id=device, device_id_type=MESH)
-
-    for partner in partners:
-        greet(tm=partner, space=other)
-    pl.when(has_low)(lambda: greet(space=s - 1))
-    pl.when(has_high)(lambda: greet(space=s + 1))
-    pl.when(t > 0)(lambda: greet(tm=t - 1))
+    around = [{"tm": lax.rem(z + dz, groups // 2) * 2 + y} for dz in (2, groups // 2 - 2, 1, groups // 2 - 1)]
+    flip = [{"tm": 2 * z + 1 - y}]
+    across = [{"tm": 2 * z + dy, "space": other} for dy in range(2)]
+
+    def greet(sem, devices):
+        for device in devices:
+            pl.semaphore_signal(sem, inc=1, device_id=device, device_id_type=MESH)
+
+    greet(barrier, around + across + flip)
+    pl.when(has_low)(lambda: greet(barrier, [{"space": s - 1}]))
+    pl.when(has_high)(lambda: greet(barrier, [{"space": s + 1}]))
     loads = [
         pltpu.make_async_copy(src, dst, load_sem.at[i])
         for i, (src, dst) in enumerate(
-            ((x_hbm, x_ref), (damp_hbm, damp_ref), (init_hbm, init_ref), (f_hbm, f_ref))
+            ((x_hbm, x_ref), (mix_hbm, mix_ref), (st_hbm, st_ref), (damp_hbm, damp_ref), (init_hbm, init_ref), (f_hbm, f_ref))
         )
     ]
     for load in loads:
@@ -185,12 +189,13 @@
 
     loads[0].wait()
     lax.fori_loop(0, NG * GC, split, 0)
-    loads[1].wait()
-    loads[2].wait()
+    for load in loads[1:5]:
+        load.wait()
     lax.fori_loop(0, NG * GC, rates, 0)
-    loads[3].wait()
-    edges = has_low.astype(jnp.int32) + has_high.astype(jnp.int32) + (t < groups - 1).astype(jnp.int32)
-    pl.semaphore_wait(barrier, groups + edges)
+    loads[5].wait()
+    edges = has_low.astype(jnp.int32) + has_high.astype(jnp.int32)
+    pl.semaphore_wait(barrier, len(around + across + flip) + edges)
+    greet(second, around + across)
 
     for g in range(NG):
         x_sides(g)[0]()
@@ -198,13 +203,11 @@
     constants(1).start()
 
     def previous(h):
-        some = pl.ds(6 * h, 6)
+        some = pl.ds(CUT * h, CUT + h * (NG * GC - 2 * CUT))
         return pltpu.make_async_remote_copy(
             x_ref.at[1, some], prev.at[some], prev_send.at[h], prev_recv.at[h],
             device_id={"tm": t + 1}, device_id_type=MESH,
         )
-
-    pl.when(t < groups - 1)(lambda: previous(0).start())
 
     for side, exists in ((0, has_low), (1, has_high)):
 
@@ -234,6 +237,9 @@
                 aside[n, g, i, at] = tile(turned)
         return 0
 
+    pl.semaphore_wait(second, len(around + across))
+    greet(third, around)
+    pl.when(t < groups - 1)(lambda: previous(0).start())
     lax.fori_loop(0, NG * GC, defects_inside, 0, unroll=UNROLL)
 
     def defects(g, _):
@@ -260,6 +266,7 @@
             return 0
 
         lax.fori_loop(0, GC, channel, 0, unroll=UNROLL)
+        pl.when(g == 0)(lambda: pl.semaphore_wait(third, len(around)))
         gather(e, r, 0, g)
         return 0
 
@@ -407,7 +414,6 @@
 
 def body(forcing, iterate, initial_state, damping, mixing, stencil):
     vmem = pl.BlockSpec(memory_space=pltpu.VMEM)
-    smem = pl.BlockSpec(memory_space=pltpu.SMEM)
     hbm = pl.BlockSpec(memory_space=pltpu.HBM)
 
     def field(*lead):
@@ -421,13 +427,15 @@
 
     slots = pltpu.VMEM((NG, 16, 8, LANES), jnp.float32)
     dma = pltpu.SemaphoreType.DMA
-    updated, defect = pl.pallas_call(
+    results = pl.pallas_call(
         kernel,
-        out_shape=[rows(2)] * 2,
-        in_specs=[hbm] * 4 + [smem] * 2,
-        out_specs=[vmem] * 2,
+        out_shape=rows(2, 2),
+        in_specs=[hbm] * 6,
+        out_specs=vmem,
         scratch_shapes=[
-            rows(2), rows(2), rows(), rows(), dma((4,)),
+            rows(2), rows(2), rows(), rows(),
+            pltpu.SMEM((NG * GC, NG * GC), jnp.float32), pltpu.SMEM((NG * GC, 26), jnp.float32), dma((6,)),
+            pltpu.SemaphoreType.REGULAR, pltpu.SemaphoreType.REGULAR,
             field(2), field(2), pltpu.VMEM((2, NG, 8, LANES), jnp.float32), dma((2,)), dma((2,)),
             field(2), face(2, 2), field(), face(2), field(),
             rows(),
@@ -446,7 +454,7 @@
             collective_id=0, has_side_effects=True, vmem_limit_bytes=60 * 1024 * 1024
         ),
     )(rows_of(forcing), rows_of(iterate), rows_of(initial_state), rows_of(damping), mixing, stencil.T)
-    return planes_of(updated), planes_of(defect)
+    return planes_of(results[0]), planes_of(results[1])
 
 
 def solution(mesh):

time: 46.4 us -> 44.2 us (0.953); the launches traced: 45.8 us -> 44.1 us
  Pallas kernels: 43.7 us -> 42.6 us
  local copies, waits for them, and re-layouts: 1.49 us -> 0.93 us
    unnamed x2 -> x0, local copies, waits for them, and re-layouts: 1.49 us -> none
    pallas_call x1, Pallas kernels: 43.7 us -> 42.6 us  [body(): pl.pallas_call(kernel, out_shape=rows(2, 2), in_specs=[hbm] * 6, out_spec...]
    slice x0 -> x1, local copies, waits for them, and re-layouts: none -> 0.93 us  [body(): return (planes_of(results[0]), planes_of(results[1]))]
where the time goes in v3:
time: 44.2 us; the launch traced here: 44.1 us
  Pallas kernels  42.6 us (96%)
  local copies, waits for them, and re-layouts  0.93 us (2%)
  between operations  0.64 us (1%)
    pallas_call x1, Pallas kernels, body(): pl.pallas_call(kernel, out_shape=rows(2, 2), in_specs=[hbm] * 6, out_spec...  42.6 us
    slice x1, local copies, waits for them, and re-layouts, body(): return (planes_of(results[0]), planes_of(results[1]))  0.93 us

profile of v3, /device:TPU:8, one launch (start us, length us, event | category | flops | bytes accessed | tf_op | source)
XLA Modules:
  0.0 44.1 jit_solution(14954145062273859935)
XLA Ops:
  0.6 42.6 %shard_map.77 = f32[2,2,12,32,128]{4,3,2,1,0:T(8,128)S(1)} custom-call(f32[2,12,32,128]{3,2,1,0:T(8,128)} %bitcast.33, f32[2,12,32,128]{3,2,1,0:T(8,128)} %bitcast.34, f32[12,32,128]{2,1,0:T(8,128)} %bitcast.35, f32[12,32,128]{2,1,0:T(8,128)} %bitcast.36, f32[12,12]{1,0:T(8,128)} %mix_hbm.1, f32[12,26]{1,0:T(8,128)} %bitcast.37), custom_call_target="tpu_custom_call" | custom-call | tf_op jit(solution)/shard_map/pallas_call | solution.py:430
  43.2 0.9 %fusion = (f32[1,2,12,32,128]{4,3,2,1,0:T(8,128)}, f32[1,2,12,32,128]{4,3,2,1,0:T(8,128)}) fusion(f32[2,2,12,32,128]{4,3,2,1,0:T(8,128)S(1)} %shard_map.77), kind=kLoop, calls=%fused_computation | loop fusion | bytes 1572864 | tf_op jit(solution)/shard_map/slice | solution.py:457

commit v4 on v3

--- a/solution.py
+++ b/solution.py
@@ -106,8 +106,9 @@
             )
 
         def start():
-            pl.when(has_low)(lambda: low().start())
+            pl.when(has_low & (s % 2 == 0))(lambda: low().start())
             pl.when(has_high)(lambda: high().start())
+            pl.when(has_low & (s % 2 == 1))(lambda: low().start())
 
         def wait_recv():
             pl.when(has_low)(lambda: high().wait_recv())
@@ -208,6 +209,9 @@
             x_ref.at[1, some], prev.at[some], prev_send.at[h], prev_recv.at[h],
             device_id={"tm": t + 1}, device_id_type=MESH,
         )
+
+    pl.when((t < groups - 1) & (y == 0))(lambda: previous(0).start())
+
 
     for side, exists in ((0, has_low), (1, has_high)):
 
@@ -239,7 +243,7 @@
 
     pl.semaphore_wait(second, len(around + across))
     greet(third, around)
-    pl.when(t < groups - 1)(lambda: previous(0).start())
+    pl.when((t < groups - 1) & (y == 1))(lambda: previous(0).start())
     lax.fori_loop(0, NG * GC, defects_inside, 0, unroll=UNROLL)
 
     def defects(g, _):

time: 44.2 us -> 43.8 us (level)
  Pallas kernels: 42.6 us -> 42.1 us
where the time goes in v4:
time: 43.8 us; the launch traced here: 43.7 us
  Pallas kernels  42.1 us (96%)
  local copies, waits for them, and re-layouts  0.93 us (2%)
  between operations  0.64 us (1%)
    pallas_call x1, Pallas kernels, body(): pl.pallas_call(kernel, out_shape=rows(2, 2), in_specs=[hbm] * 6, out_spec...  42.1 us
    slice x1, local copies, waits for them, and re-layouts, body(): return (planes_of(results[0]), planes_of(results[1]))  0.93 us

profile of v4, /device:TPU:8, one launch (start us, length us, event | category | flops | bytes accessed | tf_op | source)
XLA Modules:
  0.0 43.7 jit_solution(2146244624876676789)
XLA Ops:
  0.6 42.1 %shard_map.77 = f32[2,2,12,32,128]{4,3,2,1,0:T(8,128)S(1)} custom-call(f32[2,12,32,128]{3,2,1,0:T(8,128)} %bitcast.33, f32[2,12,32,128]{3,2,1,0:T(8,128)} %bitcast.34, f32[12,32,128]{2,1,0:T(8,128)} %bitcast.35, f32[12,32,128]{2,1,0:T(8,128)} %bitcast.36, f32[12,12]{1,0:T(8,128)} %mix_hbm.1, f32[12,26]{1,0:T(8,128)} %bitcast.37), custom_call_target="tpu_custom_call" | custom-call | tf_op jit(solution)/shard_map/pallas_call | solution.py:434
  42.8 0.9 %fusion = (f32[1,2,12,32,128]{4,3,2,1,0:T(8,128)}, f32[1,2,12,32,128]{4,3,2,1,0:T(8,128)}) fusion(f32[2,2,12,32,128]{4,3,2,1,0:T(8,128)S(1)} %shard_map.77), kind=kLoop, calls=%fused_computation | loop fusion | bytes 1572864 | tf_op jit(solution)/shard_map/slice | solution.py:461

commit v5 on v4

--- a/solution.py
+++ b/solution.py
@@ -42,11 +42,15 @@
     flip = [{"tm": 2 * z + 1 - y}]
     across = [{"tm": 2 * z + dy, "space": other} for dy in range(2)]
 
+    aslant = [
+        {"tm": lax.rem(z + dz, groups // 2) * 2 + dy, "space": other} for dz in (1, groups // 2 - 1) for dy in range(2)
+    ]
+
     def greet(sem, devices):
         for device in devices:
             pl.semaphore_signal(sem, inc=1, device_id=device, device_id_type=MESH)
 
-    greet(barrier, around + across + flip)
+    greet(barrier, around + aslant + across + flip)
     pl.when(has_low)(lambda: greet(barrier, [{"space": s - 1}]))
     pl.when(has_high)(lambda: greet(barrier, [{"space": s + 1}]))
     loads = [
@@ -195,7 +199,7 @@
     lax.fori_loop(0, NG * GC, rates, 0)
     loads[5].wait()
     edges = has_low.astype(jnp.int32) + has_high.astype(jnp.int32)
-    pl.semaphore_wait(barrier, len(around + across + flip) + edges)
+    pl.semaphore_wait(barrier, len(around + aslant + across + flip) + edges)
     greet(second, around + across)
 
     for g in range(NG):
@@ -242,7 +246,7 @@
         return 0
 
     pl.semaphore_wait(second, len(around + across))
-    greet(third, around)
+    greet(third, around[2:])
     pl.when((t < groups - 1) & (y == 1))(lambda: previous(0).start())
     lax.fori_loop(0, NG * GC, defects_inside, 0, unroll=UNROLL)
 
@@ -270,7 +274,7 @@
             return 0
 
         lax.fori_loop(0, GC, channel, 0, unroll=UNROLL)
-        pl.when(g == 0)(lambda: pl.semaphore_wait(third, len(around)))
+        pl.when(g == 0)(lambda: pl.semaphore_wait(third, len(around[2:])))
         gather(e, r, 0, g)
         return 0
 

time: 43.8 us -> 43.9 us (level)
  no operation moved by 1% of the time
where the time goes in v5:
time: 43.9 us; the launch traced here: 43.5 us
  Pallas kernels  41.9 us (95%)
  local copies, waits for them, and re-layouts  0.93 us (2%)
  between operations  0.64 us (1%)
    pallas_call x1, Pallas kernels, body(): pl.pallas_call(kernel, out_shape=rows(2, 2), in_specs=[hbm] * 6, out_spec...  41.9 us
    slice x1, local copies, waits for them, and re-layouts, body(): return (planes_of(results[0]), planes_of(results[1]))  0.93 us

profile of v5, /device:TPU:8, one launch (start us, length us, event | category | flops | bytes accessed | tf_op | source)
XLA Modules:
  0.0 43.5 jit_solution(5059177946701767179)
XLA Ops:
  0.6 41.9 %shard_map.77 = f32[2,2,12,32,128]{4,3,2,1,0:T(8,128)S(1)} custom-call(f32[2,12,32,128]{3,2,1,0:T(8,128)} %bitcast.33, f32[2,12,32,128]{3,2,1,0:T(8,128)} %bitcast.34, f32[12,32,128]{2,1,0:T(8,128)} %bitcast.35, f32[12,32,128]{2,1,0:T(8,128)} %bitcast.36, f32[12,12]{1,0:T(8,128)} %mix_hbm.1, f32[12,26]{1,0:T(8,128)} %bitcast.37), custom_call_target="tpu_custom_call" | custom-call | tf_op jit(solution)/shard_map/pallas_call | solution.py:438
  42.6 0.9 %fusion = (f32[1,2,12,32,128]{4,3,2,1,0:T(8,128)}, f32[1,2,12,32,128]{4,3,2,1,0:T(8,128)}) fusion(f32[2,2,12,32,128]{4,3,2,1,0:T(8,128)S(1)} %shard_map.77), kind=kLoop, calls=%fused_computation | loop fusion | bytes 1572864 | tf_op jit(solution)/shard_map/slice | solution.py:465
